TPU v7x, 256 devices: a whole 4x4x8 slice. The times are simulated.
256 devices in a mesh: row: 16 (over z, core), col: 8 (over y_hi, x), rep: 2 (over y_lo).
Axes of the slice: x: 4, y: 4 (y_hi: 2, y_lo: 2; y = y_hi * 2 + y_lo), z: 8, core: 2. Of those that a mesh axis runs over, the one named last changes fastest.
Arguments:
- node_features: bfloat16 [65536, 256], P(('row', 'col', 'rep')), may hold values from -6 to 6
- weight: bfloat16 [256, 256], replicated, may hold values from -0.375 to 0.375
- cotangent: bfloat16 [65536, 256], P(('col', 'rep', 'row')), may hold values from -6 to 6
- adjacency_blocks: bfloat16 [16, 16, 256, 128, 128], P(('col', 'rep'), 'row'), may hold values from -0.0625 to 0.0625
- block_coords: int32 [16, 16, 2, 256], P(('col', 'rep'), 'row'), may hold values from 0 to 31, as said below
- block_counts: int32 [16, 16], P(('col', 'rep'), 'row'), may hold values from 1 to 256, as said below
Outputs:
- hidden: bfloat16 [65536, 256], P(('col', 'rep', 'row'))
- weight_grad: float32 [256, 256], replicated
- feature_grad: bfloat16 [65536, 256], P(('row', 'col', 'rep'))
Inputs may be any that keep to these rules, and one draw needn't show every extreme that they name: block_coords[i, r, 0, k] is a block row below 32 and block_coords[i, r, 1, k] a block column below 32; within a tile the first min(256, 1024) slots name distinct positions. Only the first block_counts[i, r] slots of tile (i, r) belong to the adjacency; the values and coordinates in its other slots are not part of it.
All inputs are finite; a program needn't handle non-finite values.
Results may differ from a plain program's by a relative error of at most 0.029.
Values may be sent and summed in bfloat16 or wider, within the bound.
No kernel may reach another device: no remote copies, remote signals or barrier semaphores. Data moves between devices by JAX's collectives and lax.ppermute only.
A program may use at most 128 MiB of HBM per device.

v0:
```python
import math
import jax
import jax.numpy as jnp
from jax import lax
from jax.sharding import PartitionSpec as P


def silu_slope(values):
    sigma = jax.nn.sigmoid(values)
    return sigma * (1.0 + values * (1.0 - sigma))


def tile_product(blocks, coords, filled, source, out_blocks, flipped):
    slot_total = blocks.shape[0]
    block_size = blocks.shape[1]
    feature_width = source.shape[1]
    group_size = math.gcd(slot_total, 64)
    groups = slot_total // group_size
    source_blocks = source.reshape(-1, block_size, feature_width)
    take_index = coords[0] if flipped else coords[1]
    put_index = coords[1] if flipped else coords[0]
    active = (jnp.arange(slot_total, dtype=jnp.int32) < filled).astype(jnp.float32)
    einsum_form = "kba,kbf->kaf" if flipped else "kab,kbf->kaf"
    targets = jnp.arange(out_blocks, dtype=jnp.int32)

    def accumulate(running, pieces):
        block_group, take_group, put_group, active_group = pieces
        gathered = source_blocks[take_group]
        product = jnp.einsum(einsum_form, block_group, gathered, preferred_element_type=jnp.float32)
        placing = (put_group[:, None] == targets[None, :]).astype(jnp.float32) * active_group[
            :, None
        ]
        flat = product.reshape(group_size, block_size * feature_width)
        placed = lax.dot_general(
            placing,
            flat,
            (((0,), (0,)), ((), ())),
            precision=lax.Precision.HIGHEST,
            preferred_element_type=jnp.float32,
        )
        return (running + placed, None)

    running = jnp.zeros((out_blocks, block_size * feature_width), jnp.float32)
    running, _ = lax.scan(
        accumulate,
        running,
        (
            blocks.reshape(groups, group_size, block_size, block_size),
            take_index.reshape(groups, group_size),
            put_index.reshape(groups, group_size),
            active.reshape(groups, group_size),
        ),
    )
    return running.reshape(out_blocks * block_size, feature_width)


def body(node_features, weight, cotangent, adjacency_blocks, block_coords, block_counts):
    blocks = adjacency_blocks[0, 0]
    coords = block_coords[0, 0]
    filled = block_counts[0, 0]
    block_size = blocks.shape[-1]
    local_nodes = node_features.shape[0]
    row_devices = lax.axis_size("row")
    node_total = local_nodes * row_devices * lax.axis_size("col") * lax.axis_size("rep")
    tile_rows = local_nodes * row_devices
    column_feats = lax.all_gather(node_features, ("col", "rep"), axis=0, tiled=True)
    tile_cols = column_feats.shape[0]
    partial_value = tile_product(
        blocks, coords, filled, column_feats, tile_rows // block_size, False
    )
    own_sum = lax.psum_scatter(
        partial_value.astype(jnp.bfloat16), "row", scatter_dimension=0, tiled=True
    )
    pre_act = jnp.dot(own_sum, weight, preferred_element_type=jnp.float32)
    hidden = jax.nn.silu(pre_act).astype(jnp.bfloat16)
    own_grad = (cotangent.astype(jnp.float32) * silu_slope(pre_act)).astype(jnp.bfloat16)
    own_mixed_grad = jnp.dot(own_grad, weight.T, preferred_element_type=jnp.float32).astype(
        jnp.bfloat16
    )
    panel_grad = lax.all_gather(own_mixed_grad, "row", axis=0, tiled=True)
    weight_part = lax.dot_general(
        own_sum, own_grad, (((0,), (0,)), ((), ())), preferred_element_type=jnp.float32
    )
    weight_grad = lax.psum(weight_part, ("row", "col", "rep")) / math.sqrt(node_total)
    back_terms = tile_product(blocks, coords, filled, panel_grad, tile_cols // block_size, True)
    feature_grad = lax.psum_scatter(
        back_terms.astype(jnp.bfloat16), ("col", "rep"), scatter_dimension=0, tiled=True
    )
    return (hidden, weight_grad, feature_grad)


def solution(mesh):
    in_specs = (
        P(("row", "col", "rep"), None),
        P(),
        P(("col", "rep", "row"), None),
        P(("col", "rep"), "row", None, None, None),
        P(("col", "rep"), "row", None, None),
        P(("col", "rep"), "row"),
    )
    out_specs = (P(("col", "rep", "row"), None), P(), P(("row", "col", "rep"), None))
    return jax.shard_map(body, mesh=mesh, in_specs=in_specs, out_specs=out_specs, check_vma=False)
```

profile of v0, /device:TPU:32, one launch (start us, length us, event | category | flops | bytes accessed | tf_op | source)
XLA Modules:
  0.0 642.4 jit_solution(17018396184696318942)
XLA Ops:
  9.6 81.7 %all-gather.3.cloned.1.call-done = bf16[4096,256]{1,0:T(8,128)(2,1)} async-done(((bf16[256,256]{1,0:T(8,128)(2,1)}), bf16[4096,256]{1,0:T(8,128)(2,1)}) %all-gather.3.cloned.1.call-update) | async-done | bytes 2097168 | tf_op jit(solution)/shard_map/all_gather | solution.py:66
  91.3 99.7 %while.22 = (s32[]{:T(128)}, f32[32,32768]{1,0:T(8,128)}, s32[4,64]{1,0:T(4,128)S(1)}, f32[4,64]{1,0:T(4,128)S(1)}, bf16[4,64,128,128]{3,2,1,0:T(8,128)(2,1)}, /...) while((s32[]{:T(128)}, f32[32,32768]{1,0:T(8,128)}, ...), condition=%wide.region_1.2_spmd.clone, body=%wide.region_0.1_spmd.clone.sunk | while | flops 1344279808 | bytes 56630384 | solution.py:44
  91.3 4.3 gather_fusion
  99.7 8.0 %copy.16 = f32[8,8,128,256]{3,1,2,0:T(8,128)} copy(f32[8,8,128,256]{3,2,1,0:T(8,128)S(1)} %bitcast.88) | data formatting | bytes 16777216 | tf_op jit(solution)/shard_map/while
  107.7 8.0 %convolution_add_fusion.4 = f32[32,32768]{1,0:T(8,128)} fusion(f32[64,32768]{1,0:T(8,128)} %bitcast.86, f32[32,32768]{1,0:T(8,128)} %get-tuple-element.276, pred[]{:T(512)S(6)} %compare.6, f32[64]{0:T(128)S(1)} %fusion.64, s32[64]{0:T(128)S(1)} %fusion.65), kind=kOutput, calls=%fused_computation.4.clone.1 | convolution fusion | flops 807407616 | bytes 16777728 | tf_op jit(solution)/shard_map/while/body/eval_jaxpr/dot_general | solution.py:34
  115.7 4.3 gather_fusion
  124.1 8.0 %copy.16 = f32[8,8,128,256]{3,1,2,0:T(8,128)} copy(f32[8,8,128,256]{3,2,1,0:T(8,128)S(1)} %bitcast.88) | data formatting | bytes 16777216 | tf_op jit(solution)/shard_map/while
  132.1 8.7 %convolution_add_fusion.4 = f32[32,32768]{1,0:T(8,128)} fusion(f32[64,32768]{1,0:T(8,128)} %bitcast.86, f32[32,32768]{1,0:T(8,128)} %get-tuple-element.276, pred[]{:T(512)S(6)} %compare.6, f32[64]{0:T(128)S(1)} %fusion.64, s32[64]{0:T(128)S(1)} %fusion.65), kind=kOutput, calls=%fused_computation.4.clone.1 | convolution fusion | flops 807407616 | bytes 16777728 | tf_op jit(solution)/shard_map/while/body/eval_jaxpr/dot_general | solution.py:34
  140.8 4.3 gather_fusion
  149.2 8.0 %copy.16 = f32[8,8,128,256]{3,1,2,0:T(8,128)} copy(f32[8,8,128,256]{3,2,1,0:T(8,128)S(1)} %bitcast.88) | data formatting | bytes 16777216 | tf_op jit(solution)/shard_map/while
  157.2 8.7 %convolution_add_fusion.4 = f32[32,32768]{1,0:T(8,128)} fusion(f32[64,32768]{1,0:T(8,128)} %bitcast.86, f32[32,32768]{1,0:T(8,128)} %get-tuple-element.276, pred[]{:T(512)S(6)} %compare.6, f32[64]{0:T(128)S(1)} %fusion.64, s32[64]{0:T(128)S(1)} %fusion.65), kind=kOutput, calls=%fused_computation.4.clone.1 | convolution fusion | flops 807407616 | bytes 16777728 | tf_op jit(solution)/shard_map/while/body/eval_jaxpr/dot_general | solution.py:34
  165.9 4.3 gather_fusion
  174.3 8.0 %copy.16 = f32[8,8,128,256]{3,1,2,0:T(8,128)} copy(f32[8,8,128,256]{3,2,1,0:T(8,128)S(1)} %bitcast.88) | data formatting | bytes 16777216 | tf_op jit(solution)/shard_map/while
  182.3 8.7 %convolution_add_fusion.4 = f32[32,32768]{1,0:T(8,128)} fusion(f32[64,32768]{1,0:T(8,128)} %bitcast.86, f32[32,32768]{1,0:T(8,128)} %get-tuple-element.276, pred[]{:T(512)S(6)} %compare.6, f32[64]{0:T(128)S(1)} %fusion.64, s32[64]{0:T(128)S(1)} %fusion.65), kind=kOutput, calls=%fused_computation.4.clone.1 | convolution fusion | flops 807407616 | bytes 16777728 | tf_op jit(solution)/shard_map/while/body/eval_jaxpr/dot_general | solution.py:34
  195.8 56.5 %reduce-scatter.3.cloned.1.call-done = bf16[256,256]{1,0:T(8,128)(2,1)} async-done(((bf16[4096,256]{1,0:T(8,128)(2,1)}), bf16[256,256]{1,0:T(8,128)(2,1)}) %reduce-scatter.3.cloned.1.call-update) | async-done | bytes 131088 | tf_op jit(solution)/shard_map/reduce_scatter | solution.py:71
  255.1 12.0 %copy.9 = bf16[1,1,256,128,128]{3,4,2,1,0:T(8,128)(2,1)} copy(bf16[1,1,256,128,128]{4,3,2,1,0:T(8,128)(2,1)} %bitcast.93) | data formatting | bytes 16777216 | tf_op args[3]
  268.3 27.7 %all-gather.5.cloned.1.call-done = bf16[4096,256]{1,0:T(8,128)(2,1)} async-done(((bf16[256,256]{1,0:T(8,128)(2,1)}), bf16[4096,256]{1,0:T(8,128)(2,1)}) %all-gather.5.cloned.1.call-update) | async-done | bytes 2097168 | tf_op jit(solution)/shard_map/all_gather | solution.py:80
  296.0 99.8 %while.23 = (s32[]{:T(128)}, f32[32,32768]{1,0:T(8,128)}, s32[4,64]{1,0:T(4,128)S(1)}, f32[4,64]{1,0:T(4,128)S(1)}, bf16[4,64,128,128]{2,3,1,0:T(8,128)(2,1)}, /...) while((s32[]{:T(128)}, f32[32,32768]{1,0:T(8,128)}, ...), condition=%wide.region_5.6_spmd.clone, body=%wide.region_4.5_spmd.clone.sunk | while | flops 1344279808 | bytes 56630384 | solution.py:44
  296.0 4.4 gather_fusion.1
  304.5 8.0 %copy.17 = f32[8,8,128,256]{3,1,2,0:T(8,128)} copy(f32[8,8,128,256]{3,2,1,0:T(8,128)S(1)} %bitcast.89) | data formatting | bytes 16777216 | tf_op jit(solution)/shard_map/while
  312.4 8.0 %convolution_add_fusion.5 = f32[32,32768]{1,0:T(8,128)} fusion(f32[64,32768]{1,0:T(8,128)} %bitcast.87, f32[32,32768]{1,0:T(8,128)} %get-tuple-element.303, pred[]{:T(512)S(6)} %compare.7, f32[64]{0:T(128)S(1)} %fusion.72, s32[64]{0:T(128)S(1)} %fusion.73), kind=kOutput, calls=%fused_computation.24.clone.1 | convolution fusion | flops 807407616 | bytes 16777728 | tf_op jit(solution)/shard_map/while/body/eval_jaxpr/dot_general | solution.py:34
  320.4 4.4 gather_fusion.1
  328.9 8.0 %copy.17 = f32[8,8,128,256]{3,1,2,0:T(8,128)} copy(f32[8,8,128,256]{3,2,1,0:T(8,128)S(1)} %bitcast.89) | data formatting | bytes 16777216 | tf_op jit(solution)/shard_map/while
  336.9 8.7 %convolution_add_fusion.5 = f32[32,32768]{1,0:T(8,128)} fusion(f32[64,32768]{1,0:T(8,128)} %bitcast.87, f32[32,32768]{1,0:T(8,128)} %get-tuple-element.303, pred[]{:T(512)S(6)} %compare.7, f32[64]{0:T(128)S(1)} %fusion.72, s32[64]{0:T(128)S(1)} %fusion.73), kind=kOutput, calls=%fused_computation.24.clone.1 | convolution fusion | flops 807407616 | bytes 16777728 | tf_op jit(solution)/shard_map/while/body/eval_jaxpr/dot_general | solution.py:34
  345.6 4.4 gather_fusion.1
  354.1 8.0 %copy.17 = f32[8,8,128,256]{3,1,2,0:T(8,128)} copy(f32[8,8,128,256]{3,2,1,0:T(8,128)S(1)} %bitcast.89) | data formatting | bytes 16777216 | tf_op jit(solution)/shard_map/while
  362.0 8.6 %convolution_add_fusion.5 = f32[32,32768]{1,0:T(8,128)} fusion(f32[64,32768]{1,0:T(8,128)} %bitcast.87, f32[32,32768]{1,0:T(8,128)} %get-tuple-element.303, pred[]{:T(512)S(6)} %compare.7, f32[64]{0:T(128)S(1)} %fusion.72, s32[64]{0:T(128)S(1)} %fusion.73), kind=kOutput, calls=%fused_computation.24.clone.1 | convolution fusion | flops 807407616 | bytes 16777728 | tf_op jit(solution)/shard_map/while/body/eval_jaxpr/dot_general | solution.py:34
  370.7 4.4 gather_fusion.1
  379.2 8.0 %copy.17 = f32[8,8,128,256]{3,1,2,0:T(8,128)} copy(f32[8,8,128,256]{3,2,1,0:T(8,128)S(1)} %bitcast.89) | data formatting | bytes 16777216 | tf_op jit(solution)/shard_map/while
  387.1 8.7 %convolution_add_fusion.5 = f32[32,32768]{1,0:T(8,128)} fusion(f32[64,32768]{1,0:T(8,128)} %bitcast.87, f32[32,32768]{1,0:T(8,128)} %get-tuple-element.303, pred[]{:T(512)S(6)} %compare.7, f32[64]{0:T(128)S(1)} %fusion.72, s32[64]{0:T(128)S(1)} %fusion.73), kind=kOutput, calls=%fused_computation.24.clone.1 | convolution fusion | flops 807407616 | bytes 16777728 | tf_op jit(solution)/shard_map/while/body/eval_jaxpr/dot_general | solution.py:34
  400.6 148.2 %all-reduce.2.cloned.1.call-done = f32[256,256]{1,0:T(8,128)} async-done(((f32[256,256]{1,0:T(8,128)}), f32[256,256]{1,0:T(8,128)}) %all-reduce.2.cloned.1.call-update) | async-done | bytes 262160 | tf_op jit(solution)/shard_map/psum | solution.py:84
  550.5 85.3 %reduce-scatter.5.cloned.1.call-done = bf16[256,256]{1,0:T(8,128)(2,1)} async-done(((bf16[4096,256]{1,0:T(8,128)(2,1)}), bf16[256,256]{1,0:T(8,128)(2,1)}) %reduce-scatter.5.cloned.1.call-update) | async-done | bytes 131088 | tf_op jit(solution)/shard_map/reduce_scatter | solution.py:86
  (72 shorter events, 49.7 us)
Async XLA Ops:
  7.2 245.1 %copy-start = (bf16[256,256]{1,0:T(8,128)(2,1)S(1)}, bf16[256,256]{1,0:T(8,128)(2,1)}, u32[]{:S(2)}) copy-start(bf16[256,256]{1,0:T(8,128)(2,1)} %param.11) | copy-start | bytes 393220
  7.2 84.1 %all-gather.3.cloned.1.call-start = ((), (), s32[]{:S(2)}) async-start(), calls=%async_computation.2 | async-start | bytes 2228224 | tf_op jit(solution)/shard_map/all_gather | solution.py:66
  7.9 244.4 %reduce-scatter.3.cloned.1.call-start = ((), (), s32[]{:S(2)}) async-start(), calls=%async_computation.3 | async-start | bytes 2228224 | tf_op jit(solution)/shard_map/reduce_scatter | solution.py:71
  193.4 58.9 %copy-start.3 = (bf16[256,256]{1,0:T(8,128)(2,1)S(1)}, bf16[256,256]{1,0:T(8,128)(2,1)}, u32[]{:S(2)}) copy-start(bf16[256,256]{1,0:T(8,128)(2,1)} %param.12) | copy-start | bytes 393220
  195.8 100.3 %all-gather.5.cloned.1.call-start = ((), (), s32[]{:S(2)}) async-start(), calls=%async_computation.5 | async-start | bytes 2228224 | tf_op jit(solution)/shard_map/all_gather | solution.py:80
  255.0 12.1 %copy-start.2 = (bf16[256,256]{1,0:T(8,128)(2,1)S(1)}, bf16[256,256]{1,0:T(8,128)(2,1)}, u32[]{:S(2)}) copy-start(bf16[256,256]{1,0:T(8,128)(2,1)} %reduce-scatter.3.cloned.1.call-done) | copy-start | bytes 393220
  255.0 293.8 %all-reduce.2.cloned.1.call-start = ((), (), s32[]{:S(2)}) async-start(), calls=%async_computation.4 | async-start | bytes 524288 | tf_op jit(solution)/shard_map/psum | solution.py:84
  268.1 367.8 %reduce-scatter.5.cloned.1.call-start = ((), (), s32[]{:S(2)}) async-start(), calls=%async_computation.6 | async-start | bytes 2228224 | tf_op jit(solution)/shard_map/reduce_scatter | solution.py:86
  395.8 240.0 %copy-start.1 = (bf16[256,256]{1,0:T(8,128)(2,1)S(1)}, bf16[256,256]{1,0:T(8,128)(2,1)}, u32[]{:S(2)}) copy-start(bf16[256,256]{1,0:T(8,128)(2,1)} %param.11) | copy-start | bytes 393220
Sparse Core Ops, SparseCore 0:
  9.8 81.4 all-gather.2
  195.9 56.3 reduce-scatter.2
  255.2 40.8 all-gather.4
  301.9 246.9 all-reduce.1
  551.8 83.9 reduce-scatter.4
where the time goes:
time: 643 us; the launch traced here: 642 us
  waiting for transfers between devices  400 us (62%)
  local copies, waits for them, and re-layouts  116 us (18%)
  matrix products  104 us (16%)
  between operations  14.5 us (2%)
  other arithmetic  6.61 us (1%)
    psum x1, waiting for transfers between devices, body(): lax.psum(weight_part, ('row', 'col', 'rep')) / math.sqrt(node_total)  148 us
    reduce_scatter x1, waiting for transfers between devices, body(): lax.psum_scatter(back_terms.astype(jnp.bfloat16), ('col', 'rep'), scatter...  85.3 us
    all_gather x1, waiting for transfers between devices, body(): lax.all_gather(node_features, ('col', 'rep'), axis=0, tiled=True)  81.7 us
    dot_general x8, matrix products, accumulate(): lax.dot_general(placing, flat, (((0,), (0,)), ((), ())), precision=lax.Pr...  68 us
    while x8, local copies, waits for them, and re-layouts  63.7 us
    reduce_scatter x1, waiting for transfers between devices, body(): lax.psum_scatter(partial_value.astype(jnp.bfloat16), 'row', scatter_dimen...  56.5 us
    gather x8, local copies, waits for them, and re-layouts, accumulate(): gathered = source_blocks[take_group]  34.8 us
    dot_general x8, matrix products, accumulate(): jnp.einsum(einsum_form, block_group, gathered, preferred_element_type=jnp...  32.6 us
  transfers between devices with their start and end apart: 5, of which 5 were waited for; matrix products, arithmetic and copies ran while one was open for 19% of the time, Pallas kernels for 0%

commit v1 on v0

--- a/solution.py
+++ b/solution.py
@@ -81,7 +81,7 @@
     weight_part = lax.dot_general(
         own_sum, own_grad, (((0,), (0,)), ((), ())), preferred_element_type=jnp.float32
     )
-    weight_grad = lax.psum(weight_part, ("row", "col", "rep")) / math.sqrt(node_total)
+    weight_grad = lax.psum(lax.psum(weight_part, "row"), ("col", "rep")) / math.sqrt(node_total)
     back_terms = tile_product(blocks, coords, filled, panel_grad, tile_cols // block_size, True)
     feature_grad = lax.psum_scatter(
         back_terms.astype(jnp.bfloat16), ("col", "rep"), scatter_dimension=0, tiled=True

time: 643 us -> 603 us (0.938)
  waiting for transfers between devices: 400 us -> 359 us
    psum x1 -> x2, waiting for transfers between devices: 148 us -> 94.9 us  [the longest x1 94.8 us: body(): lax.psum(weight_part, 'row')]
    all_gather x1, waiting for transfers between devices: 27.7 us -> 44.1 us  [body(): panel_grad = lax.all_gather(own_mixed_grad, 'row', axis=0, tiled=True)]
  transfers between devices with their start and end apart: 5 -> 6, of which waited for: 5 -> 5; matrix products, arithmetic and copies ran while one was open for 19% -> 20% of each run, Pallas kernels for 0% -> 0%
where the time goes in v1:
time: 603 us; the launch traced here: 602 us
  waiting for transfers between devices  359 us (60%)
  local copies, waits for them, and re-layouts  116 us (19%)
  matrix products  105 us (17%)
  between operations  14.8 us (2%)
  other arithmetic  6.61 us (1%)
    psum x1, waiting for transfers between devices, body(): lax.psum(weight_part, 'row')  94.8 us
    all_gather x1, waiting for transfers between devices, body(): lax.all_gather(node_features, ('col', 'rep'), axis=0, tiled=True)  81.7 us
    reduce_scatter x1, waiting for transfers between devices, body(): lax.psum_scatter(back_terms.astype(jnp.bfloat16), ('col', 'rep'), scatter...  80.7 us
    dot_general x8, matrix products, accumulate(): lax.dot_general(placing, flat, (((0,), (0,)), ((), ())), precision=lax.Pr...  68.1 us
    while x8, local copies, waits for them, and re-layouts  63.7 us
    reduce_scatter x1, waiting for transfers between devices, body(): lax.psum_scatter(partial_value.astype(jnp.bfloat16), 'row', scatter_dimen...  56.7 us
    all_gather x1, waiting for transfers between devices, body(): panel_grad = lax.all_gather(own_mixed_grad, 'row', axis=0, tiled=True)  44.1 us
    gather x8, local copies, waits for them, and re-layouts, accumulate(): gathered = source_blocks[take_group]  34.9 us
  transfers between devices with their start and end apart: 6, of which 5 were waited for; matrix products, arithmetic and copies ran while one was open for 20% of the time, Pallas kernels for 0%

profile of v1, /device:TPU:32, one launch (start us, length us, event | category | flops | bytes accessed | tf_op | source)
XLA Modules:
  0.0 602.1 jit_solution(7835479593575485644)
XLA Ops:
  9.6 81.7 %all-gather.3.cloned.1.call-done = bf16[4096,256]{1,0:T(8,128)(2,1)} async-done(((bf16[256,256]{1,0:T(8,128)(2,1)}), bf16[4096,256]{1,0:T(8,128)(2,1)}) %all-gather.3.cloned.1.call-update) | async-done | bytes 2097168 | tf_op jit(solution)/shard_map/all_gather | solution.py:66
  91.3 99.8 %while.22 = (s32[]{:T(128)}, f32[32,32768]{1,0:T(8,128)}, s32[4,64]{1,0:T(4,128)S(1)}, f32[4,64]{1,0:T(4,128)S(1)}, bf16[4,64,128,128]{3,2,1,0:T(8,128)(2,1)}, /...) while((s32[]{:T(128)}, f32[32,32768]{1,0:T(8,128)}, ...), condition=%wide.region_1.2_spmd.clone, body=%wide.region_0.1_spmd.clone.sunk | while | flops 1344279808 | bytes 56630384 | solution.py:44
  91.3 4.3 gather_fusion
  99.7 8.0 %copy.16 = f32[8,8,128,256]{3,1,2,0:T(8,128)} copy(f32[8,8,128,256]{3,2,1,0:T(8,128)S(1)} %bitcast.88) | data formatting | bytes 16777216 | tf_op jit(solution)/shard_map/while
  107.7 8.0 %convolution_add_fusion.4 = f32[32,32768]{1,0:T(8,128)} fusion(f32[64,32768]{1,0:T(8,128)} %bitcast.86, f32[32,32768]{1,0:T(8,128)} %get-tuple-element.276, pred[]{:T(512)S(6)} %compare.6, f32[64]{0:T(128)S(1)} %fusion.64, s32[64]{0:T(128)S(1)} %fusion.65), kind=kOutput, calls=%fused_computation.4.clone.1 | convolution fusion | flops 807407616 | bytes 16777728 | tf_op jit(solution)/shard_map/while/body/eval_jaxpr/dot_general | solution.py:34
  115.8 4.3 gather_fusion
  124.2 8.0 %copy.16 = f32[8,8,128,256]{3,1,2,0:T(8,128)} copy(f32[8,8,128,256]{3,2,1,0:T(8,128)S(1)} %bitcast.88) | data formatting | bytes 16777216 | tf_op jit(solution)/shard_map/while
  132.1 8.7 %convolution_add_fusion.4 = f32[32,32768]{1,0:T(8,128)} fusion(f32[64,32768]{1,0:T(8,128)} %bitcast.86, f32[32,32768]{1,0:T(8,128)} %get-tuple-element.276, pred[]{:T(512)S(6)} %compare.6, f32[64]{0:T(128)S(1)} %fusion.64, s32[64]{0:T(128)S(1)} %fusion.65), kind=kOutput, calls=%fused_computation.4.clone.1 | convolution fusion | flops 807407616 | bytes 16777728 | tf_op jit(solution)/shard_map/while/body/eval_jaxpr/dot_general | solution.py:34
  140.9 4.3 gather_fusion
  149.3 8.0 %copy.16 = f32[8,8,128,256]{3,1,2,0:T(8,128)} copy(f32[8,8,128,256]{3,2,1,0:T(8,128)S(1)} %bitcast.88) | data formatting | bytes 16777216 | tf_op jit(solution)/shard_map/while
  157.3 8.7 %convolution_add_fusion.4 = f32[32,32768]{1,0:T(8,128)} fusion(f32[64,32768]{1,0:T(8,128)} %bitcast.86, f32[32,32768]{1,0:T(8,128)} %get-tuple-element.276, pred[]{:T(512)S(6)} %compare.6, f32[64]{0:T(128)S(1)} %fusion.64, s32[64]{0:T(128)S(1)} %fusion.65), kind=kOutput, calls=%fused_computation.4.clone.1 | convolution fusion | flops 807407616 | bytes 16777728 | tf_op jit(solution)/shard_map/while/body/eval_jaxpr/dot_general | solution.py:34
  166.0 4.3 gather_fusion
  174.4 8.0 %copy.16 = f32[8,8,128,256]{3,1,2,0:T(8,128)} copy(f32[8,8,128,256]{3,2,1,0:T(8,128)S(1)} %bitcast.88) | data formatting | bytes 16777216 | tf_op jit(solution)/shard_map/while
  182.4 8.7 %convolution_add_fusion.4 = f32[32,32768]{1,0:T(8,128)} fusion(f32[64,32768]{1,0:T(8,128)} %bitcast.86, f32[32,32768]{1,0:T(8,128)} %get-tuple-element.276, pred[]{:T(512)S(6)} %compare.6, f32[64]{0:T(128)S(1)} %fusion.64, s32[64]{0:T(128)S(1)} %fusion.65), kind=kOutput, calls=%fused_computation.4.clone.1 | convolution fusion | flops 807407616 | bytes 16777728 | tf_op jit(solution)/shard_map/while/body/eval_jaxpr/dot_general | solution.py:34
  195.9 56.7 %reduce-scatter.3.cloned.1.call-done = bf16[256,256]{1,0:T(8,128)(2,1)} async-done(((bf16[4096,256]{1,0:T(8,128)(2,1)}), bf16[256,256]{1,0:T(8,128)(2,1)}) %reduce-scatter.3.cloned.1.call-update) | async-done | bytes 131088 | tf_op jit(solution)/shard_map/reduce_scatter | solution.py:71
  257.2 12.0 %copy.9 = bf16[1,1,256,128,128]{3,4,2,1,0:T(8,128)(2,1)} copy(bf16[1,1,256,128,128]{4,3,2,1,0:T(8,128)(2,1)} %bitcast.93) | data formatting | bytes 16777216 | tf_op args[3]
  269.2 94.8 %all-reduce.3.cloned.1.call-done = f32[256,256]{1,0:T(8,128)} async-done(((f32[256,256]{1,0:T(8,128)}), f32[256,256]{1,0:T(8,128)}) %all-reduce.3.cloned.1.call-update) | async-done | bytes 262160 | tf_op jit(solution)/shard_map/psum | solution.py:84
  364.3 44.1 %all-gather.5.cloned.1.call-done = bf16[4096,256]{1,0:T(8,128)(2,1)} async-done(((bf16[256,256]{1,0:T(8,128)(2,1)}), bf16[4096,256]{1,0:T(8,128)(2,1)}) %all-gather.5.cloned.1.call-update) | async-done | bytes 2097168 | tf_op jit(solution)/shard_map/all_gather | solution.py:80
  408.4 99.7 %while.23 = (s32[]{:T(128)}, f32[32,32768]{1,0:T(8,128)}, s32[4,64]{1,0:T(4,128)S(1)}, f32[4,64]{1,0:T(4,128)S(1)}, bf16[4,64,128,128]{2,3,1,0:T(8,128)(2,1)}, /...) while((s32[]{:T(128)}, f32[32,32768]{1,0:T(8,128)}, ...), condition=%wide.region_6.7_spmd.clone, body=%wide.region_5.6_spmd.clone.sunk | while | flops 1344279808 | bytes 56630384 | solution.py:44
  408.4 4.4 gather_fusion.1
  416.8 8.0 %copy.17 = f32[8,8,128,256]{3,1,2,0:T(8,128)} copy(f32[8,8,128,256]{3,2,1,0:T(8,128)S(1)} %bitcast.89) | data formatting | bytes 16777216 | tf_op jit(solution)/shard_map/while
  424.8 8.0 %convolution_add_fusion.5 = f32[32,32768]{1,0:T(8,128)} fusion(f32[64,32768]{1,0:T(8,128)} %bitcast.87, f32[32,32768]{1,0:T(8,128)} %get-tuple-element.303, pred[]{:T(512)S(6)} %compare.7, f32[64]{0:T(128)S(1)} %fusion.72, s32[64]{0:T(128)S(1)} %fusion.73), kind=kOutput, calls=%fused_computation.24.clone.1 | convolution fusion | flops 807407616 | bytes 16777728 | tf_op jit(solution)/shard_map/while/body/eval_jaxpr/dot_general | solution.py:34
  432.8 4.4 gather_fusion.1
  441.3 8.0 %copy.17 = f32[8,8,128,256]{3,1,2,0:T(8,128)} copy(f32[8,8,128,256]{3,2,1,0:T(8,128)S(1)} %bitcast.89) | data formatting | bytes 16777216 | tf_op jit(solution)/shard_map/while
  449.3 8.7 %convolution_add_fusion.5 = f32[32,32768]{1,0:T(8,128)} fusion(f32[64,32768]{1,0:T(8,128)} %bitcast.87, f32[32,32768]{1,0:T(8,128)} %get-tuple-element.303, pred[]{:T(512)S(6)} %compare.7, f32[64]{0:T(128)S(1)} %fusion.72, s32[64]{0:T(128)S(1)} %fusion.73), kind=kOutput, calls=%fused_computation.24.clone.1 | convolution fusion | flops 807407616 | bytes 16777728 | tf_op jit(solution)/shard_map/while/body/eval_jaxpr/dot_general | solution.py:34
  457.9 4.4 gather_fusion.1
  466.4 8.0 %copy.17 = f32[8,8,128,256]{3,1,2,0:T(8,128)} copy(f32[8,8,128,256]{3,2,1,0:T(8,128)S(1)} %bitcast.89) | data formatting | bytes 16777216 | tf_op jit(solution)/shard_map/while
  474.3 8.7 %convolution_add_fusion.5 = f32[32,32768]{1,0:T(8,128)} fusion(f32[64,32768]{1,0:T(8,128)} %bitcast.87, f32[32,32768]{1,0:T(8,128)} %get-tuple-element.303, pred[]{:T(512)S(6)} %compare.7, f32[64]{0:T(128)S(1)} %fusion.72, s32[64]{0:T(128)S(1)} %fusion.73), kind=kOutput, calls=%fused_computation.24.clone.1 | convolution fusion | flops 807407616 | bytes 16777728 | tf_op jit(solution)/shard_map/while/body/eval_jaxpr/dot_general | solution.py:34
  483.0 4.4 gather_fusion.1
  491.5 8.0 %copy.17 = f32[8,8,128,256]{3,1,2,0:T(8,128)} copy(f32[8,8,128,256]{3,2,1,0:T(8,128)S(1)} %bitcast.89) | data formatting | bytes 16777216 | tf_op jit(solution)/shard_map/while
  499.4 8.7 %convolution_add_fusion.5 = f32[32,32768]{1,0:T(8,128)} fusion(f32[64,32768]{1,0:T(8,128)} %bitcast.87, f32[32,32768]{1,0:T(8,128)} %get-tuple-element.303, pred[]{:T(512)S(6)} %compare.7, f32[64]{0:T(128)S(1)} %fusion.72, s32[64]{0:T(128)S(1)} %fusion.73), kind=kOutput, calls=%fused_computation.24.clone.1 | convolution fusion | flops 807407616 | bytes 16777728 | tf_op jit(solution)/shard_map/while/body/eval_jaxpr/dot_general | solution.py:34
  514.6 80.7 %reduce-scatter.5.cloned.1.call-done = bf16[256,256]{1,0:T(8,128)(2,1)} async-done(((bf16[4096,256]{1,0:T(8,128)(2,1)}), bf16[256,256]{1,0:T(8,128)(2,1)}) %reduce-scatter.5.cloned.1.call-update) | async-done | bytes 131088 | tf_op jit(solution)/shard_map/reduce_scatter | solution.py:86
  (73 shorter events, 50.6 us)
Async XLA Ops:
  7.2 245.4 %copy-start = (bf16[256,256]{1,0:T(8,128)(2,1)S(1)}, bf16[256,256]{1,0:T(8,128)(2,1)}, u32[]{:S(2)}) copy-start(bf16[256,256]{1,0:T(8,128)(2,1)} %param.11) | copy-start | bytes 393220
  7.2 84.1 %all-gather.3.cloned.1.call-start = ((), (), s32[]{:S(2)}) async-start(), calls=%async_computation.2 | async-start | bytes 2228224 | tf_op jit(solution)/shard_map/all_gather | solution.py:66
  7.9 244.6 %reduce-scatter.3.cloned.1.call-start = ((), (), s32[]{:S(2)}) async-start(), calls=%async_computation.3 | async-start | bytes 2228224 | tf_op jit(solution)/shard_map/reduce_scatter | solution.py:71
  193.5 59.1 %copy-start.2 = (bf16[256,256]{1,0:T(8,128)(2,1)S(1)}, bf16[256,256]{1,0:T(8,128)(2,1)}, u32[]{:S(2)}) copy-start(bf16[256,256]{1,0:T(8,128)(2,1)} %param.12) | copy-start | bytes 393220
  195.8 168.2 %all-reduce.3.cloned.1.call-start = ((), (), s32[]{:S(2)}) async-start(), calls=%async_computation.4 | async-start | bytes 524288 | tf_op jit(solution)/shard_map/psum | solution.py:84
  256.2 152.1 %all-gather.5.cloned.1.call-start = ((), (), s32[]{:S(2)}) async-start(), calls=%async_computation.6 | async-start | bytes 2228224 | tf_op jit(solution)/shard_map/all_gather | solution.py:80
  257.2 255.7 %all-reduce.5.cloned.1.call-start = ((), (), s32[]{:S(2)}) async-start(), calls=%async_computation.5 | async-start | bytes 524288 | tf_op jit(solution)/shard_map/psum | solution.py:84
  364.1 231.2 %reduce-scatter.5.cloned.1.call-start = ((), (), s32[]{:S(2)}) async-start(), calls=%async_computation.7 | async-start | bytes 2228224 | tf_op jit(solution)/shard_map/reduce_scatter | solution.py:86
  508.1 87.2 %copy-start.1 = (bf16[256,256]{1,0:T(8,128)(2,1)S(1)}, bf16[256,256]{1,0:T(8,128)(2,1)}, u32[]{:S(2)}) copy-start(bf16[256,256]{1,0:T(8,128)(2,1)} %param.11) | copy-start | bytes 393220
Sparse Core Ops, SparseCore 0:
  9.8 81.4 all-gather.2
  196.0 56.5 reduce-scatter.2
  256.4 107.6 all-reduce.2
  366.5 41.8 all-gather.4
  411.7 93.3 all-reduce.4
  513.0 82.1 reduce-scatter.4
